TPU v7x, 32 devices: a whole 2x2x4 slice. The times are simulated.
32 devices in a mesh: groups: 2 (over y), dom: 4 (over z), slab: 2 (over x), sub: 2 (over core).
Axes of the slice: x: 2, y: 2, z: 4, core: 2. Of those that a mesh axis runs over, the one named last changes fastest.
Arguments:
- volume: float32 [2, 65536, 512], P(None, ('groups', 'dom', 'slab')), parts along dimension 1, may hold values from -6 to 6
- interp: bfloat16 [8, 2, 4, 512, 128], P('dom', 'slab'), may hold values from -0.09375 to 0.09375
- fetch_lists: int32 [8, 2, 4, 12], P(('groups', 'dom'), 'slab'), parts along dimension 0, may hold values from 0 to 4095, as said below
- slot_of: int32 [16, 2, 512, 4], P(('groups', 'dom'), 'slab', 'sub'), parts along dimension 0, may hold values from 0 to 47
- images: bfloat16 [1, 32, 512, 2, 128], P(None, ('groups', 'dom'), 'sub'), parts along dimension 1, may hold values from -6 to 6
- particle_bin: int32 [1, 32], P(None, ('groups', 'dom')), parts along dimension 1, may hold values from 0 to 7, as said below
- ctf_class: int32 [1, 32], P(None, ('groups', 'dom')), parts along dimension 1, may hold values from 0 to 7
- defocus: float32 [8], replicated, may hold values from 20 to 200
Outputs:
- new_volume: float32 [2, 65536, 512], P(None, ('groups', 'dom', 'slab')), parts along dimension 1
There are 2 independent parts, one for each index of `groups`. A program takes and returns all parts, laid end to end along the dimension named above; an argument that names none is the same for every part. Nothing has to cross between parts.
Inputs may be any that keep to these rules, and one draw needn't show every extreme that they name: fetch_lists[i, s, o, :] holds 12 distinct local indices of the tiles that dom index o holds in slab s. `particle_bin`: the particles of dom index i lie in bins i * 2 to (i + 1) * 2 - 1.
All inputs are finite; a program needn't handle non-finite values.
Results may differ from a plain program's by a relative error of at most 0.00044.
Values may be sent and summed in bfloat16 or wider, within the bound.
A program may use at most 128 MiB of HBM per device.

v0:
```python
import jax
import jax.numpy as jnp
from jax import lax
from jax.sharding import PartitionSpec as P

L = 256


step_rate = 0.3
phase_shift = 0.1


def radius_table(first_tile, tile_count, pixel_width):
    tile_index = first_tile + jnp.arange(tile_count, dtype=jnp.int32)
    pixels = jnp.arange(pixel_width, dtype=jnp.int32)
    row_index = tile_index * pixel_width // L
    col_start = tile_index * pixel_width % L
    rowpos = (row_index - L // 2).astype(jnp.float32)[:, None]
    colpos = (col_start[:, None] + pixels[None, :] - L // 2).astype(jnp.float32)
    return (rowpos * rowpos + colpos * colpos) / float((L // 2) ** 2)


def weigh_residual(slices, pictures, bin_local, classes, defocus, first_tile):
    tile_count = pictures.shape[1]
    pixel_width = pictures.shape[3]
    bin_count = slices.shape[0]
    radius = radius_table(first_tile, tile_count, pixel_width)
    class_match = classes[:, None] == jnp.arange(defocus.shape[0], dtype=jnp.int32)[None, :]
    focus_value = jnp.sum(jnp.where(class_match, defocus[None, :], 0.0), axis=1)
    transfer = -jnp.sin(focus_value[:, None, None] * radius[None] + phase_shift)[:, :, None, :]
    picked = jnp.take(slices, bin_local, axis=0)
    residual = transfer * picked - pictures.astype(jnp.float32)
    weighted = transfer * residual
    member = (bin_local[:, None] == jnp.arange(bin_count, dtype=jnp.int32)[None, :]).astype(
        jnp.float32
    )
    summed = jnp.einsum("pb,pjxq->bjxq", member, weighted, precision=lax.Precision.HIGHEST)
    return summed.astype(jnp.bfloat16)


def shards(volume, interp, fetch_lists, slot_of, images, particle_bin, ctf_class, defocus):
    dom_count = lax.axis_size("dom")
    wanted = fetch_lists[0, 0]
    capacity = wanted.shape[1]
    weights = interp[:, 0]
    bin_count = weights.shape[0]
    tile_width = weights.shape[2]
    references = jnp.transpose(slot_of[:, 0], (0, 2, 1))
    slot_depth = references.shape[1]
    tile_count = references.shape[2]
    flat_refs = references.reshape(-1)
    first_tile = lax.axis_index("sub") * tile_count
    asked_ids = lax.all_to_all(wanted, "dom", split_axis=0, concat_axis=0, tiled=True)
    asked_flat = asked_ids.reshape(-1)
    full_flat = asked_ids.reshape(-1)
    current = volume
    outgoing = jnp.take(current, asked_flat, axis=1).astype(jnp.bfloat16)
    outgoing = outgoing.reshape(2, dom_count, asked_ids.shape[1], tile_width)
    fetched = lax.all_to_all(outgoing, "dom", split_axis=1, concat_axis=1, tiled=True)
    fetched = fetched.reshape(2, dom_count * capacity, tile_width)
    gathered = jnp.take(fetched, flat_refs, axis=1).reshape(
        2, bin_count, slot_depth, tile_count, tile_width
    )
    partial_value = jnp.einsum(
        "xbkjv,bkvq->bjxq", gathered, weights, preferred_element_type=jnp.float32
    )
    pictures = images[0]
    bin_local = particle_bin[0] % bin_count
    classes = ctf_class[0]
    slices = lax.psum(partial_value, "slab")
    summed = weigh_residual(slices, pictures, bin_local, classes, defocus, first_tile)
    spread = jnp.einsum("bjxq,bkvq->xbkjv", summed, weights, preferred_element_type=jnp.float32)
    slot_grads = jnp.zeros((2, dom_count * capacity, tile_width), jnp.float32)
    slot_grads = slot_grads.at[:, flat_refs].add(spread.reshape(2, -1, tile_width))
    slot_grads = slot_grads.reshape(2, dom_count, capacity, tile_width)
    own_rows = lax.all_to_all(slot_grads, "dom", split_axis=1, concat_axis=1, tiled=True)
    row_grads = lax.psum(own_rows, "sub")
    current = current.at[:, full_flat].add(-step_rate * row_grads.reshape(2, -1, tile_width))
    return current


def solution(mesh):
    in_specs = (
        P(None, ("groups", "dom", "slab"), None),
        P("dom", "slab", None, None, None),
        P(("groups", "dom"), "slab", None, None),
        P(("groups", "dom"), "slab", "sub", None),
        P(None, ("groups", "dom"), "sub", None, None),
        P(None, ("groups", "dom")),
        P(None, ("groups", "dom")),
        P(),
    )
    out_specs = P(None, ("groups", "dom", "slab"), None)
    return jax.shard_map(shards, mesh=mesh, in_specs=in_specs, out_specs=out_specs, check_vma=False)
```

profile of v0, /device:TPU:0, one launch (start us, length us, event | category | flops | bytes accessed | tf_op | source)
XLA Modules:
  0.0 325.5 jit_solution(435083408074344969)
XLA Ops:
  6.5 11.9 %copy.53 = f32[2,4096,512]{2,1,0:T(8,128)} copy(f32[2,4096,512]{2,1,0:T(8,128)} %param.8) | data formatting | bytes 33554432
  18.4 6.3 %all-to-all-start = ((s32[4,1,12]{2,1,0:T(1,128)}), s32[4,1,12]{2,1,0:T(1,128)S(1)}, u32[]{:S(2)}, u32[]{:S(2)}) async-start(s32[4,1,12]{2,1,0:T(1,128)} %bitcast.1), calls=%async_computation | async-start | bytes 4096 | tf_op jit(solution)/shard_map/all_to_all | solution.py:53
  24.9 5.3 %all-to-all-done = s32[4,1,12]{2,1,0:T(1,128)S(1)} async-done(((s32[4,1,12]{2,1,0:T(1,128)}), s32[4,1,12]{2,1,0:T(1,128)S(1)}, u32[]{:S(2)}, u32[]{:S(2)}) %all-to-all-start) | async-done | bytes 224 | tf_op jit(solution)/shard_map/all_to_all | solution.py:53
  30.2 0.5 broadcast.334
  30.7 0.6 reduce.3
  31.4 2.3 gather_fusion
  33.8 0.8 select_convert_fusion
  34.6 3.3 %all-to-all-start.1 = ((bf16[2,4,12,512]{3,0,2,1:T(2,128)(2,1)}), bf16[2,4,12,512]{3,0,2,1:T(2,128)(2,1)S(1)}, u32[]{:S(2)}, u32[]{:S(2)}) async-start(bf16[2,4,12,512]{3,0,2,1:T(2,128)(2,1)} %select_convert_fusion), calls=%async_computation.1 | async-start | bytes 196608 | tf_op jit(solution)/shard_map/all_to_all | solution.py:59
  38.2 5.5 %all-to-all-done.1 = bf16[2,4,12,512]{3,0,2,1:T(2,128)(2,1)S(1)} async-done(((bf16[2,4,12,512]{3,0,2,1:T(2,128)(2,1)}), bf16[2,4,12,512]{3,0,2,1:T(2,128)(2,1)S(1)}, u32[]{:S(2)}, u32[]{:S(2)}) %all-to-all-start.1) | async-done | bytes 98336 | tf_op jit(solution)/shard_map/all_to_all | solution.py:59
  43.7 21.4 %gather_fusion.1 = bf16[2048,2,512]{2,1,0:T(2,128)(2,1)} fusion(bf16[2,48,512]{2,0,1:T(2,128)(2,1)S(1)} %bitcast.58, s32[2048]{0:T(1024)S(1)} %broadcast_clamp_fusion), kind=kCustom, calls=%fused_computation.1 | custom fusion | bytes 8396800 | tf_op jit(solution)/shard_map/jit(_take)/gather | solution.py:61
  65.1 4.3 %fusion.3 = f32[2,256,2,128]{3,1,2,0:T(8,128)} fusion(bf16[2,2,4,256,512]{4,0,3,2,1:T(2,128)(2,1)} %bitcast.60, pred[2,4,256]{2,1,0:T(4,128)(4,1)S(1)} %compare_and_fusion, bf16[2,1,4,512,128]{4,3,2,1,0:T(8,128)(2,1)S(1)} %copy-done), kind=kOutput, calls=%fused_computation.10 | convolution fusion | flops 538968064 | bytes 5769216 | tf_op jit(solution)/shard_map/xbkjv,bkvq->bjxq/dot_general | solution.py:64
  69.8 1.8 sine_negate_fusion
  71.6 25.3 %all-reduce.3.cloned.1.call-done = f32[2,256,2,128]{3,1,2,0:T(8,128)} async-done(((f32[2,256,2,128]{3,1,2,0:T(8,128)}), f32[2,256,2,128]{3,1,2,0:T(8,128)}) %all-reduce.3.cloned.1.call-update) | async-done | bytes 524304 | tf_op jit(solution)/shard_map/psum | solution.py:70
  97.0 1.7 gather_fusion.2
  98.6 0.2 fusion.5
  98.9 1.7 fusion.4
  100.6 1.3 convolution_bitcast_fusion
  101.8 1.3 copy.30
  103.2 16.5 %copy.31 = f32[2048,2,512]{2,1,0:T(2,128)} copy(f32[2048,2,512]{2,0,1:T(8,128)S(1)} %bitcast.59) | data formatting | bytes 16777216 | tf_op jit(solution)/shard_map/reshape | solution.py:74
  119.8 162.3 %scatter_fusion = f32[2,48,512]{2,0,1:T(2,128)S(1)} fusion(f32[2,48,512]{2,0,1:T(2,128)S(1)} %broadcast_in_dim.57, s32[2048]{0:T(1024)S(1)} %bitcast.65, f32[2048,2,512]{2,1,0:T(2,128)} %copy.31), kind=kCustom, calls=%fused_computation.3 | custom fusion | flops 2097152 | bytes 25174016 | tf_op jit(solution)/shard_map/scatter-add | solution.py:74
  282.0 12.0 %all_to_all.19 = f32[2,4,12,512]{3,0,2,1:T(2,128)} all-to-all(f32[2,4,12,512]{3,0,2,1:T(2,128)S(1)} %bitcast.57), channel_id=1, replica_groups=mesh['groups'=2,'dom'=4,'slab'=2,'sub'=2] {'dom'}, dimensions={1} | all-to-all | bytes 393216 | tf_op jit(solution)/shard_map/all_to_all | solution.py:76
  294.1 16.4 %all-reduce.5.cloned.1.call-done = f32[2,4,12,512]{3,0,2,1:T(2,128)} async-done(((f32[2,4,12,512]{3,0,2,1:T(2,128)}), f32[2,4,12,512]{3,0,2,1:T(2,128)}) %all-reduce.5.cloned.1.call-update) | async-done | bytes 196624 | tf_op jit(solution)/shard_map/psum | solution.py:77
  310.5 1.0 broadcast_multiply_fusion
  311.5 7.1 %scatter_fusion.1 = f32[2,4096,512]{2,1,0:T(8,128)} fusion(f32[2,4096,512]{2,1,0:T(8,128)} %copy.53, s32[48]{0:T(128)S(1)} %fusion.16, f32[48,2,512]{2,0,1:T(8,128)S(1)} %copy.32), kind=kCustom, calls=%fused_computation.4 | custom fusion | flops 49152 | bytes 590016 | tf_op jit(solution)/shard_map/scatter-add | solution.py:78
  (36 shorter events, 1.0 us)
Async XLA Ops:
  6.5 58.6 %copy-start = (bf16[2,1,4,512,128]{4,3,2,1,0:T(8,128)(2,1)S(1)}, bf16[2,1,4,512,128]{4,3,2,1,0:T(8,128)(2,1)}, u32[]{:S(2)}) copy-start(bf16[2,1,4,512,128]{4,3,2,1,0:T(8,128)(2,1)} %param.9) | copy-start | bytes 3145732
  6.5 18.3 %copy-start.3 = (s32[2,1,256,4]{2,3,1,0:T(4,128)S(1)}, s32[2,1,256,4]{2,3,1,0:T(4,128)}, u32[]{:S(2)}) copy-start(s32[2,1,256,4]{2,3,1,0:T(4,128)} %param.11) | copy-start | bytes 24580
  6.5 18.2 %copy-start.4 = (s32[1,4]{1,0:T(1,128)S(1)}, s32[1,4]{1,0:T(1,128)}, u32[]{:S(2)}) copy-start(s32[1,4]{1,0:T(1,128)} %param.13) | copy-start | bytes 52
  6.5 31.5 %copy-start.6 = (s32[1,4]{1,0:T(1,128)S(1)}, s32[1,4]{1,0:T(1,128)}, u32[]{:S(2)}) copy-start(s32[1,4]{1,0:T(1,128)} %param.14) | copy-start | bytes 52
  6.5 31.5 %copy-start.5 = (f32[8]{0:T(128)S(1)}, f32[8]{0:T(128)}, u32[]{:S(2)}) copy-start(f32[8]{0:T(128)} %param.15) | copy-start | bytes 100
  18.4 11.8 %all-to-all-start = ((s32[4,1,12]{2,1,0:T(1,128)}), s32[4,1,12]{2,1,0:T(1,128)S(1)}, u32[]{:S(2)}, u32[]{:S(2)}) async-start(s32[4,1,12]{2,1,0:T(1,128)} %bitcast.1), calls=%async_computation | async-start | bytes 4096 | tf_op jit(solution)/shard_map/all_to_all | solution.py:53
  34.6 9.1 %all-to-all-start.1 = ((bf16[2,4,12,512]{3,0,2,1:T(2,128)(2,1)}), bf16[2,4,12,512]{3,0,2,1:T(2,128)(2,1)S(1)}, u32[]{:S(2)}, u32[]{:S(2)}) async-start(bf16[2,4,12,512]{3,0,2,1:T(2,128)(2,1)} %select_convert_fusion), calls=%async_computation.1 | async-start | bytes 196608 | tf_op jit(solution)/shard_map/all_to_all | solution.py:59
  37.9 59.0 %all-reduce.3.cloned.1.call-start = ((), (), s32[]{:S(2)}) async-start(), calls=%async_computation.3 | async-start | bytes 1048576 | tf_op jit(solution)/shard_map/psum | solution.py:70
  65.1 33.5 %copy-start.2 = (bf16[1,4,256,2,128]{4,3,2,1,0:T(2,128)(2,1)S(1)}, bf16[1,4,256,2,128]{4,3,2,1,0:T(2,128)(2,1)}, u32[]{:S(2)}) copy-start(bf16[1,4,256,2,128]{4,3,2,1,0:T(2,128)(2,1)} %param.12) | copy-start | bytes 1572868
  69.4 241.0 %all-reduce.5.cloned.1.call-start = ((), (), s32[]{:S(2)}) async-start(), calls=%async_computation.4 | async-start | bytes 393216 | tf_op jit(solution)/shard_map/psum | solution.py:77
  119.8 198.9 %copy-start.1 = (bf16[2,1,4,512,128]{4,3,2,1,0:T(8,128)(2,1)S(1)}, bf16[2,1,4,512,128]{4,3,2,1,0:T(8,128)(2,1)}, u32[]{:S(2)}) copy-start(bf16[2,1,4,512,128]{4,3,2,1,0:T(8,128)(2,1)} %param.9) | copy-start | bytes 3145732
Sparse Core Ops, SparseCore 0:
  69.6 27.3 all-reduce.2
  294.2 16.2 all-reduce.4
where the time goes:
time: 332 us; the launch traced here: 325 us
  other arithmetic  174 us (52%)
  local copies, waits for them, and re-layouts  55.9 us (17%)
  waiting for transfers between devices  52.6 us (16%)
  between operations  13.6 us (4%)
  blocking collectives  12 us (4%)
  starting transfers between devices  9.89 us (3%)
  matrix products  7.23 us (2%)
    scatter-add x1, other arithmetic, shards(): slot_grads.at[:, flat_refs].add(spread.reshape(2, -1, tile_width))  162 us
    psum x1, waiting for transfers between devices, shards(): slices = lax.psum(partial_value, 'slab')  25.3 us
    gather x1, local copies, waits for them, and re-layouts, shards(): jnp.take(fetched, flat_refs, axis=1)  21.4 us
    reshape x1, local copies, waits for them, and re-layouts, shards(): spread.reshape(2, -1, tile_width)  16.5 us
    psum x1, waiting for transfers between devices, shards(): row_grads = lax.psum(own_rows, 'sub')  16.4 us
    all_to_all x1, blocking collectives, shards(): lax.all_to_all(slot_grads, 'dom', split_axis=1, concat_axis=1, tiled=True)  12 us
    unnamed x15, local copies, waits for them, and re-layouts  11.9 us
    scatter-add x1, other arithmetic, shards(): current.at[:, full_flat]  7.11 us
  transfers between devices with their start and end apart: 4, of which 4 were waited for; matrix products, arithmetic and copies ran while one was open for 1% of the time, Pallas kernels for 0%

commit v1 on v0

v1 whole, which is shorter than its diff:
```python
import jax
import jax.numpy as jnp
from jax import lax
from jax.sharding import PartitionSpec as P

L = 256


step_rate = 0.3
phase_shift = 0.1


def radius_table(first_tile, tile_count, pixel_width):
    tile_index = first_tile + jnp.arange(tile_count, dtype=jnp.int32)
    pixels = jnp.arange(pixel_width, dtype=jnp.int32)
    row_index = tile_index * pixel_width // L
    col_start = tile_index * pixel_width % L
    rowpos = (row_index - L // 2).astype(jnp.float32)[:, None]
    colpos = (col_start[:, None] + pixels[None, :] - L // 2).astype(jnp.float32)
    return (rowpos * rowpos + colpos * colpos) / float((L // 2) ** 2)


def weigh_residual(slices, pictures, bin_local, classes, defocus, first_tile):
    tile_count = pictures.shape[1]
    pixel_width = pictures.shape[3]
    bin_count = slices.shape[0]
    radius = radius_table(first_tile, tile_count, pixel_width)
    class_match = classes[:, None] == jnp.arange(defocus.shape[0], dtype=jnp.int32)[None, :]
    focus_value = jnp.sum(jnp.where(class_match, defocus[None, :], 0.0), axis=1)
    transfer = -jnp.sin(focus_value[:, None, None] * radius[None] + phase_shift)[:, :, None, :]
    total = [0.0] * bin_count
    for p in range(pictures.shape[0]):
        picked = slices[0]
        for b in range(1, bin_count):
            picked = jnp.where(bin_local[p] == b, slices[b], picked)
        weighted = transfer[p] * (transfer[p] * picked - pictures[p].astype(jnp.float32))
        for b in range(bin_count):
            total[b] = total[b] + jnp.where(bin_local[p] == b, weighted, 0.0)
    return jnp.stack(total).astype(jnp.bfloat16)


def halves(x, n):
    parts = []
    for _ in range(n):
        part = x.astype(jnp.bfloat16)
        x = x - part.astype(jnp.float32)
        parts.append(part)
    return parts


def shards(volume, interp, fetch_lists, slot_of, images, particle_bin, ctf_class, defocus):
    dom_count = lax.axis_size("dom")
    wanted = fetch_lists[0, 0]
    capacity = wanted.shape[1]
    weights = interp[:, 0]
    bin_count = weights.shape[0]
    tile_width = weights.shape[2]
    slots = slot_of[:, 0]
    tile_count = slots.shape[1]
    listed = dom_count * capacity
    first_tile = lax.axis_index("sub") * tile_count
    asked_ids = lax.all_to_all(wanted, "dom", split_axis=0, concat_axis=0, tiled=True)
    asked_flat = asked_ids.reshape(-1)
    outgoing = jnp.take(volume, asked_flat, axis=1).astype(jnp.bfloat16)
    outgoing = outgoing.reshape(2, dom_count, capacity, tile_width)
    fetched = lax.all_to_all(outgoing, "dom", split_axis=1, concat_axis=1, tiled=True)
    fetched = fetched.reshape(2, listed, tile_width)
    table = jnp.einsum("xmv,bkvq->bkmxq", fetched, weights, preferred_element_type=jnp.float32)
    onehot = (slots[..., None] == jnp.arange(listed, dtype=jnp.int32)).astype(jnp.bfloat16)
    partial_value = sum(
        jnp.einsum("bjkm,bkmxq->bjxq", onehot, part, preferred_element_type=jnp.float32)
        for part in halves(table, 3)
    )
    pictures = images[0]
    bin_local = particle_bin[0] % bin_count
    slices = lax.psum(partial_value, "slab")
    summed = weigh_residual(slices, pictures, bin_local, ctf_class[0], defocus, first_tile)
    slot_sum = jnp.einsum("bjkm,bjxq->bkmxq", onehot, summed, preferred_element_type=jnp.float32)
    slot_grads = sum(
        jnp.einsum("bkmxq,bkvq->xmv", part, weights, preferred_element_type=jnp.float32)
        for part in halves(slot_sum, 3)
    )
    slot_grads = slot_grads.reshape(2, dom_count, capacity, tile_width)
    own_rows = lax.all_to_all(slot_grads, "dom", split_axis=1, concat_axis=1, tiled=True)
    row_grads = lax.psum(own_rows, "sub")
    return volume.at[:, asked_flat].add(-step_rate * row_grads.reshape(2, -1, tile_width))


def solution(mesh):
    in_specs = (
        P(None, ("groups", "dom", "slab"), None),
        P("dom", "slab", None, None, None),
        P(("groups", "dom"), "slab", None, None),
        P(("groups", "dom"), "slab", "sub", None),
        P(None, ("groups", "dom"), "sub", None, None),
        P(None, ("groups", "dom")),
        P(None, ("groups", "dom")),
        P(),
    )
    out_specs = P(None, ("groups", "dom", "slab"), None)
    return jax.shard_map(shards, mesh=mesh, in_specs=in_specs, out_specs=out_specs, check_vma=False)
```

time: 332 us -> 122 us (0.37); the launches traced: 325 us -> 121 us
  other arithmetic: 174 us -> 14.2 us
  local copies, waits for them, and re-layouts: 55.9 us -> 16.4 us
  waiting for transfers between devices: 52.6 us -> 46.8 us
  between operations: 13.6 us -> 18.6 us
  matrix products: 7.23 us -> 3.74 us
    scatter-add x2 -> x1, other arithmetic: 169 us -> 7.11 us  [shards(): volume.at[:, asked_flat]]
    gather x4 -> x2, local copies, waits for them, and re-layouts: 25.5 us -> 2.4 us  [shards(): outgoing = jnp.take(volume, asked_flat, axis=1).astype(jnp.bfloat16)]
    reshape x3 -> x1, local copies, waits for them, and re-layouts: 16.6 us -> 0.09 us  [shards(): asked_flat = asked_ids.reshape(-1)]
    psum x1, waiting for transfers between devices: 25.3 us -> 21.4 us  [shards(): slices = lax.psum(partial_value, 'slab')]
    dot_general x3 -> x8, matrix products: 7.23 us -> 3.74 us  [the longest x3 1.86 us: shards(): jnp.einsum('bjkm,bkmxq->bjxq', onehot, part, preferred_element_type=jnp.f...]
    unnamed x15 -> x13, local copies, waits for them, and re-layouts: 11.9 us -> 12.1 us
  transfers between devices with their start and end apart: 4 -> 4, of which waited for: 4 -> 4; matrix products, arithmetic and copies ran while one was open for 1% -> 3% of each run, Pallas kernels for 0% -> 0%
where the time goes in v1:
time: 122 us; the launch traced here: 121 us
  waiting for transfers between devices  46.8 us (38%)
  between operations  18.6 us (15%)
  local copies, waits for them, and re-layouts  16.4 us (13%)
  other arithmetic  14.2 us (12%)
  blocking collectives  12 us (10%)
  starting transfers between devices  9.7 us (8%)
  matrix products  3.74 us (3%)
    psum x1, waiting for transfers between devices, shards(): slices = lax.psum(partial_value, 'slab')  21.4 us
    psum x1, waiting for transfers between devices, shards(): row_grads = lax.psum(own_rows, 'sub')  16.4 us
    unnamed x13, local copies, waits for them, and re-layouts  12.1 us
    all_to_all x1, blocking collectives, shards(): lax.all_to_all(slot_grads, 'dom', split_axis=1, concat_axis=1, tiled=True)  12 us
    scatter-add x1, other arithmetic, shards(): volume.at[:, asked_flat]  7.11 us
    all_to_all x1, starting transfers between devices, shards(): lax.all_to_all(wanted, 'dom', split_axis=0, concat_axis=0, tiled=True)  6.32 us
    all_to_all x1, waiting for transfers between devices, shards(): lax.all_to_all(outgoing, 'dom', split_axis=1, concat_axis=1, tiled=True)  5.72 us
    all_to_all x1, waiting for transfers between devices, shards(): lax.all_to_all(wanted, 'dom', split_axis=0, concat_axis=0, tiled=True)  3.3 us
  transfers between devices with their start and end apart: 4, of which 4 were waited for; matrix products, arithmetic and copies ran while one was open for 3% of the time, Pallas kernels for 0%

profile of v1, /device:TPU:0, one launch (start us, length us, event | category | flops | bytes accessed | tf_op | source)
XLA Modules:
  0.0 121.4 jit_solution(3953763670893732270)
XLA Ops:
  6.6 12.1 %copy.116 = f32[2,4096,512]{2,1,0:T(8,128)} copy(f32[2,4096,512]{2,1,0:T(8,128)} %param.8) | data formatting | bytes 33554432
  18.6 6.3 %all-to-all-start = ((s32[4,1,12]{2,1,0:T(1,128)}), s32[4,1,12]{2,1,0:T(1,128)S(1)}, u32[]{:S(2)}, u32[]{:S(2)}) async-start(s32[4,1,12]{2,1,0:T(1,128)} %bitcast.1), calls=%async_computation | async-start | bytes 4096 | tf_op jit(solution)/shard_map/all_to_all | solution.py:62
  25.3 1.8 %sine_negate_fusion = f32[4,256,1,128]{3,1,2,0:T(8,128)S(1)} fusion(f32[256,128]{1,0:T(8,128)S(1)} %add_multiply_fusion, f32[4]{0:T(128)S(1)} %select_reduce_fusion), kind=kLoop, calls=%fused_computation.18 | loop fusion | flops 393216 | bytes 655376 | tf_op jit(solution)/shard_map/neg | solution.py:30
  27.1 3.3 %all-to-all-done = s32[4,1,12]{2,1,0:T(1,128)S(1)} async-done(((s32[4,1,12]{2,1,0:T(1,128)}), s32[4,1,12]{2,1,0:T(1,128)S(1)}, u32[]{:S(2)}, u32[]{:S(2)}) %all-to-all-start) | async-done | bytes 224 | tf_op jit(solution)/shard_map/all_to_all | solution.py:62
  30.4 0.5 broadcast.254
  30.9 0.6 reduce.3
  31.6 2.3 %gather_fusion = bf16[48,2,512]{2,0,1:T(8,128)(2,1)S(1)} fusion(f32[2,4096,512]{2,1,0:T(8,128)} %copy.116, s32[1024]{0:T(1024)S(1)} %pad_clamp_fusion), kind=kCustom, calls=%fused_computation | custom fusion | bytes 196800 | tf_op jit(solution)/shard_map/jit(_take)/gather | solution.py:64
  34.0 0.8 select_convert_fusion
  34.8 3.3 %all-to-all-start.1 = ((bf16[2,4,12,512]{3,0,2,1:T(2,128)(2,1)}), bf16[2,4,12,512]{3,0,2,1:T(2,128)(2,1)S(1)}, u32[]{:S(2)}, u32[]{:S(2)}) async-start(bf16[2,4,12,512]{3,0,2,1:T(2,128)(2,1)} %select_convert_fusion), calls=%async_computation.1 | async-start | bytes 196608 | tf_op jit(solution)/shard_map/all_to_all | solution.py:66
  38.2 5.7 %all-to-all-done.1 = bf16[2,4,12,512]{3,0,2,1:T(2,128)(2,1)S(1)} async-done(((bf16[2,4,12,512]{3,0,2,1:T(2,128)(2,1)}), bf16[2,4,12,512]{3,0,2,1:T(2,128)(2,1)S(1)}, u32[]{:S(2)}, u32[]{:S(2)}) %all-to-all-start.1) | async-done | bytes 98336 | tf_op jit(solution)/shard_map/all_to_all | solution.py:66
  44.3 0.4 convolution_bitcast_fusion
  45.0 1.1 fusion.1
  46.2 0.7 fusion.40
  51.9 0.4 fusion.38
  52.3 21.4 %all-reduce.3.cloned.1.call-done = f32[2,256,2,128]{3,1,2,0:T(8,128)} async-done(((f32[2,256,2,128]{3,1,2,0:T(8,128)}), f32[2,256,2,128]{3,1,2,0:T(8,128)}) %all-reduce.3.cloned.1.call-update) | async-done | bytes 524304 | tf_op jit(solution)/shard_map/psum | solution.py:76
  73.7 1.3 %add_convert_fusion = bf16[1,256,2,128]{3,1,2,0:T(8,128)(2,1)S(1)} fusion(pred[]{:T(512)} %bitcast.38, pred[]{:T(512)} %bitcast.34, pred[]{:T(512)} %bitcast.30, pred[]{:T(512)} %bitcast.10, bf16[1,1,256,2,128]{4,3,2,1,0:T(2,128)(2,1)S(1)} %get-tuple-element.12, f32[2,256,2,128]{3,1,2,0:T(8,128)} %all-reduce.3.cloned.1.call-done, ...), kind=kLoop, calls=%fused_computation.41 | loop fusion | flops 1835008 | bytes 1703940 | tf_op jit(solution)/shard_map/convert.5
  74.9 1.3 %add_convert_fusion.1 = bf16[1,256,2,128]{3,1,2,0:T(8,128)(2,1)S(1)} fusion(pred[]{:T(512)} %bitcast.36, pred[]{:T(512)} %bitcast.32, pred[]{:T(512)} %bitcast.28, pred[]{:T(512)} %bitcast.7, bf16[1,1,256,2,128]{4,3,2,1,0:T(2,128)(2,1)S(1)} %get-tuple-element.12, f32[2,256,2,128]{3,1,2,0:T(8,128)} %all-reduce.3.cloned.1.call-done, pred[]{:T(512)} %bitcast.10, ...), kind=kLoop, calls=%fused_computation.42 | loop fusion | flops 1835008 | bytes 1703944 | tf_op jit(solution)/shard_map/convert.4
  76.4 0.4 convolution_bitcast_fusion.4
  76.9 0.4 convolution_bitcast_fusion.5
  77.3 0.5 fusion.4
  78.0 12.0 %all_to_all.19 = f32[2,4,12,512]{3,0,2,1:T(2,128)} all-to-all(f32[2,4,12,512]{3,0,2,1:T(2,128)S(1)} %bitcast.136), channel_id=1, replica_groups=mesh['groups'=2,'dom'=4,'slab'=2,'sub'=2] {'dom'}, dimensions={1} | all-to-all | bytes 393216 | tf_op jit(solution)/shard_map/all_to_all | solution.py:84
  90.0 16.4 %all-reduce.5.cloned.1.call-done = f32[2,4,12,512]{3,0,2,1:T(2,128)} async-done(((f32[2,4,12,512]{3,0,2,1:T(2,128)}), f32[2,4,12,512]{3,0,2,1:T(2,128)}) %all-reduce.5.cloned.1.call-update) | async-done | bytes 196624 | tf_op jit(solution)/shard_map/psum | solution.py:85
  106.3 1.0 broadcast_multiply_fusion
  107.4 7.1 %scatter_fusion = f32[2,4096,512]{2,1,0:T(8,128)} fusion(f32[2,4096,512]{2,1,0:T(8,128)} %copy.116, s32[48]{0:T(128)S(1)} %fusion.36, f32[48,2,512]{2,0,1:T(8,128)S(1)} %copy.56), kind=kCustom, calls=%fused_computation.1 | custom fusion | flops 49152 | bytes 590016 | tf_op jit(solution)/shard_map/scatter-add | solution.py:86
  (32 shorter events, 1.8 us)
Async XLA Ops:
  6.5 37.4 %copy-start = (bf16[2,1,4,512,128]{4,3,2,1,0:T(8,128)(2,1)S(1)}, bf16[2,1,4,512,128]{4,3,2,1,0:T(8,128)(2,1)}, u32[]{:S(2)}) copy-start(bf16[2,1,4,512,128]{4,3,2,1,0:T(8,128)(2,1)} %param.9) | copy-start | bytes 3145732
  6.5 37.7 %copy-start.2 = (s32[2,1,256,4]{2,3,1,0:T(4,128)S(1)}, s32[2,1,256,4]{2,3,1,0:T(4,128)}, u32[]{:S(2)}) copy-start(s32[2,1,256,4]{2,3,1,0:T(4,128)} %param.11) | copy-start | bytes 24580
  6.5 45.4 %copy-start.1 = (bf16[1,4,256,2,128]{4,3,2,1,0:T(2,128)(2,1)S(1)}, bf16[1,4,256,2,128]{4,3,2,1,0:T(2,128)(2,1)}, u32[]{:S(2)}) copy-start(bf16[1,4,256,2,128]{4,3,2,1,0:T(2,128)(2,1)} %param.12) | copy-start | bytes 1572868
  6.5 31.6 %copy-start.5 = (s32[1,4]{1,0:T(1,128)S(1)}, s32[1,4]{1,0:T(1,128)}, u32[]{:S(2)}) copy-start(s32[1,4]{1,0:T(1,128)} %param.13) | copy-start | bytes 52
  6.5 18.5 %copy-start.4 = (s32[1,4]{1,0:T(1,128)S(1)}, s32[1,4]{1,0:T(1,128)}, u32[]{:S(2)}) copy-start(s32[1,4]{1,0:T(1,128)} %param.14) | copy-start | bytes 52
  6.5 18.5 %copy-start.3 = (f32[8]{0:T(128)S(1)}, f32[8]{0:T(128)}, u32[]{:S(2)}) copy-start(f32[8]{0:T(128)} %param.15) | copy-start | bytes 100
  18.6 11.8 %all-to-all-start = ((s32[4,1,12]{2,1,0:T(1,128)}), s32[4,1,12]{2,1,0:T(1,128)S(1)}, u32[]{:S(2)}, u32[]{:S(2)}) async-start(s32[4,1,12]{2,1,0:T(1,128)} %bitcast.1), calls=%async_computation | async-start | bytes 4096 | tf_op jit(solution)/shard_map/all_to_all | solution.py:62
  34.8 9.1 %all-to-all-start.1 = ((bf16[2,4,12,512]{3,0,2,1:T(2,128)(2,1)}), bf16[2,4,12,512]{3,0,2,1:T(2,128)(2,1)S(1)}, u32[]{:S(2)}, u32[]{:S(2)}) async-start(bf16[2,4,12,512]{3,0,2,1:T(2,128)(2,1)} %select_convert_fusion), calls=%async_computation.1 | async-start | bytes 196608 | tf_op jit(solution)/shard_map/all_to_all | solution.py:66
  38.1 35.5 %all-reduce.3.cloned.1.call-start = ((), (), s32[]{:S(2)}) async-start(), calls=%async_computation.3 | async-start | bytes 1048576 | tf_op jit(solution)/shard_map/psum | solution.py:76
  46.2 60.2 %all-reduce.5.cloned.1.call-start = ((), (), s32[]{:S(2)}) async-start(), calls=%async_computation.4 | async-start | bytes 393216 | tf_op jit(solution)/shard_map/psum | solution.py:85
Sparse Core Ops, SparseCore 0:
  46.3 27.3 all-reduce.2
  90.1 16.1 all-reduce.4
